TPU v7x, 512 devices: a whole 4x4x16 slice. The times are simulated.
512 devices in a mesh: grp: 16 (over x, y), dev: 32 (over z, core).
Axes of the slice: x: 4, y: 4, z: 16, core: 2. Of those that a mesh axis runs over, the one named last changes fastest.
Arguments:
- records: bfloat16 [131072, 128], P('grp', 'dev')
- dropout: int32 [131072, 128], P('grp', 'dev'), may hold values 0 or 1
- counts: int32 [512], P(('grp', 'dev')), may hold values from 128 to 256, as said below
Outputs:
- upper: float32 [512, 512], replicated
- basis: bfloat16 [131072, 512], P(('grp', 'dev'))
Inputs may be any that keep to these rules, and one draw needn't show every extreme that they name: `counts`: at least one time shard has all 256 rows valid.
All inputs are finite; a program needn't handle non-finite values. No bound on the sum of `dropout` on one device may be relied on, other than what follows from the above.
Results may differ from a plain program's by a relative error of at most 0.0012.
Values may be sent and summed in bfloat16 or wider, within the bound.
No kernel may reach another device: no remote copies, remote signals or barrier semaphores. Data moves between devices by JAX's collectives and lax.ppermute only.
A program may use at most 128 MiB of HBM per device.

v0:
```python
import jax
import jax.numpy as jnp
from jax import lax
from jax.sharding import PartitionSpec as P

LAGS = 4


def from_behind(value, axis, by):
    size = lax.axis_size(axis)
    pairs = [(i, i + by) for i in range(size) if 0 <= i + by < size]
    return lax.ppermute(value, axis, pairs)


def gram_term(piece):
    return lax.dot_general(
        piece, piece, (((0,), (0,)), ((), ())), preferred_element_type=jnp.float32
    )


def project(piece, high, low):
    first = jnp.dot(piece, high, preferred_element_type=jnp.float32)
    second = jnp.dot(piece, low, preferred_element_type=jnp.float32)
    return (first + second).astype(jnp.bfloat16)


def exact_dot(left, right):
    return jnp.dot(left, right, precision=lax.Precision.HIGHEST)


def factor_block(block):
    size = block.shape[0]
    augmented = jnp.concatenate([block, jnp.eye(size, dtype=jnp.float32)], axis=1)
    order = jnp.arange(size, dtype=jnp.int32)

    def eliminate(step, state):
        working, written = state
        pivot_row = lax.dynamic_slice_in_dim(working, step, 1, 0)[0]
        pivot = lax.dynamic_slice_in_dim(pivot_row, step, 1, 0)[0]
        scaled = pivot_row / jnp.sqrt(pivot)
        column = lax.dynamic_slice_in_dim(working, step, 1, 1)[:, 0]
        factor = jnp.where(order > step, column / pivot, jnp.zeros_like(column))
        working = working - factor[:, None] * pivot_row[None, :]
        written = lax.dynamic_update_slice_in_dim(written, scaled[None, :], step, 0)
        return (working, written)

    _, written = lax.fori_loop(0, size, eliminate, (augmented, jnp.zeros_like(augmented)))
    upper_block = jnp.triu(written[:, :size])
    lower_inverse = jnp.tril(written[:, size:])
    return (upper_block, lower_inverse)


def factor_parts(matrix):
    size = matrix.shape[0]
    panel = min(128, size)
    panels = size // panel
    working = matrix
    diag_blocks = []
    diag_inverses = []
    right_blocks = []
    for number in range(panels):
        upper_block, lower_inverse = factor_block(working[:panel, :panel])
        beside = exact_dot(lower_inverse, working[:panel, panel:])
        working = working[panel:, panel:] - exact_dot(jnp.transpose(beside), beside)
        diag_blocks.append(upper_block)
        diag_inverses.append(jnp.transpose(lower_inverse))
        right_blocks.append(beside)
    block_rows = []
    for number in range(panels):
        pieces = []
        if number > 0:
            pieces.append(jnp.zeros((panel, number * panel), jnp.float32))
        pieces.append(diag_blocks[number])
        if number + 1 < panels:
            pieces.append(right_blocks[number])
        block_rows.append(jnp.concatenate(pieces, axis=1))
    upper = jnp.concatenate(block_rows, axis=0)
    solved = [[None] * panels for number in range(panels)]
    for column in range(panels):
        solved[column][column] = diag_inverses[column]
        for row in range(column - 1, -1, -1):
            accum = jnp.zeros((panel, panel), jnp.float32)
            for middle in range(row + 1, column + 1):
                coupling = upper[
                    row * panel : (row + 1) * panel, middle * panel : (middle + 1) * panel
                ]
                accum = accum + exact_dot(coupling, solved[middle][column])
            solved[row][column] = -exact_dot(diag_inverses[row], accum)
    inverse_rows = []
    for row in range(panels):
        pieces = []
        for column in range(panels):
            if column < row:
                pieces.append(jnp.zeros((panel, panel), jnp.float32))
            else:
                pieces.append(solved[row][column])
        inverse_rows.append(jnp.concatenate(pieces, axis=1))
    return (upper, jnp.concatenate(inverse_rows, axis=0))


def shards(records, dropout, counts):
    local = (records.astype(jnp.float32) * dropout.astype(jnp.float32)).astype(jnp.bfloat16)
    series = lax.all_to_all(local, "dev", split_axis=0, concat_axis=1, tiled=True)
    rows = series.shape[0]
    ahead = from_behind(series[: LAGS - 1], ("grp", "dev"), -1)
    padded = jnp.concatenate([series, ahead], axis=0)
    hankel = jnp.concatenate([padded[k : k + rows] for k in range(LAGS)], axis=1)
    valid = jnp.arange(rows, dtype=jnp.int32) >= rows - counts[0]
    hankel = jnp.where(valid[:, None], hankel, jnp.zeros_like(hankel))
    total_rows = rows * lax.axis_size("grp") * lax.axis_size("dev")
    partial_value = gram_term(hankel)
    gram = lax.psum(partial_value, ("grp", "dev"))
    upper, inverse = factor_parts(gram / total_rows)
    high = inverse.astype(jnp.bfloat16)
    low = (inverse - lax.optimization_barrier(high).astype(jnp.float32)).astype(jnp.bfloat16)
    basis = project(hankel, high, low)
    return (upper, basis)


def solution(mesh):
    in_specs = (P("grp", "dev"), P("grp", "dev"), P(("grp", "dev")))
    out_specs = (P(), P(("grp", "dev"), None))
    return jax.shard_map(shards, mesh=mesh, in_specs=in_specs, out_specs=out_specs, check_vma=False)
```

profile of v0, /device:TPU:1, one launch (start us, length us, event | category | flops | bytes accessed | tf_op | source)
XLA Modules:
  0.0 1999.9 jit_solution(4296532873974421739)
XLA Ops:
  7.2 1.6 multiply_convert_fusion
  8.7 16.8 all-to-all-start
  26.2 12.4 all-to-all-done
  38.6 3.5 collective-permute-start
  42.1 1.7 collective-permute-done
  44.0 1.3 fusion.66
  45.4 462.2 %all-reduce.3.cloned.1.call-done = f32[512,512]{1,0:T(8,128)} async-done(((f32[512,512]{1,0:T(8,128)}), f32[512,512]{1,0:T(8,128)}) %all-reduce.3.cloned.1.call-update) | async-done | bytes 1048592 | tf_op jit(solution)/shard_map/psum | solution.py:112
  507.6 1.3 broadcast_multiply_fusion
  509.1 368.6 %while.76 = (s32[]{:T(128)}, f32[128,256]{0,1:T(8,128)S(1)}, f32[128,256]{0,1:T(8,128)S(1)}, s32[]{:T(128)}, s32[]{:T(128)}, /*index=5*/s32[]{:T(128)}, s32[]{:T(128)}) while((s32[]{:T(128)}, f32[128,256]{0,1:T(8,128)S(1)}, f32[128,256]{0,1:T(8,128)S(1)}, s32[]{:T(128)}, s32[]{:T(128)}, /*index=5*/s32[]{:T(128)}, s32[]{:T(128)}) %tuple.188), condition=%wide.region_2.3_spmd.clone, body=%wide.region_1.2_spmd.clone.sunk | while | flops 66180 | bytes 271501 | solution.py:47
  513.9 0.7 fusion.92
  522.6 0.7 fusion.92
  531.2 0.7 fusion.92
  539.8 0.7 fusion.92
  542.7 0.7 fusion.92
  548.5 0.7 fusion.92
  551.4 0.7 fusion.92
  560.0 0.7 fusion.92
  568.7 0.7 fusion.92
  577.3 0.7 fusion.92
  585.9 0.7 fusion.92
  594.6 0.7 fusion.92
  597.5 0.7 fusion.92
  603.2 0.7 fusion.92
  606.1 0.7 fusion.92
  614.7 0.7 fusion.92
  623.4 0.7 fusion.92
  878.0 0.7 convolution_subtract_fusion
  878.9 368.6 %while.77 = (s32[]{:T(128)}, f32[128,256]{0,1:T(8,128)S(1)}, f32[128,256]{0,1:T(8,128)S(1)}, s32[]{:T(128)}, s32[]{:T(128)}, /*index=5*/s32[]{:T(128)}, s32[]{:T(128)}) while((s32[]{:T(128)}, f32[128,256]{0,1:T(8,128)S(1)}, f32[128,256]{0,1:T(8,128)S(1)}, s32[]{:T(128)}, s32[]{:T(128)}, /*index=5*/s32[]{:T(128)}, s32[]{:T(128)}) %tuple.191), condition=%wide.region_4.5_spmd.clone, body=%wide.region_3.4_spmd.clone.sunk | while | flops 66180 | bytes 271501 | solution.py:47
  1248.6 368.6 %while.78 = (s32[]{:T(128)}, f32[128,256]{0,1:T(8,128)S(1)}, f32[128,256]{0,1:T(8,128)S(1)}, s32[]{:T(128)}, s32[]{:T(128)}, /*index=5*/s32[]{:T(128)}, s32[]{:T(128)}) while((s32[]{:T(128)}, f32[128,256]{0,1:T(8,128)S(1)}, f32[128,256]{0,1:T(8,128)S(1)}, s32[]{:T(128)}, s32[]{:T(128)}, /*index=5*/s32[]{:T(128)}, s32[]{:T(128)}) %tuple.194), condition=%wide.region_6.7_spmd.clone, body=%wide.region_5.6_spmd.clone.sunk | while | flops 66180 | bytes 271501 | solution.py:47
  1618.2 368.6 %while.79 = (s32[]{:T(128)}, f32[128,256]{0,1:T(8,128)S(1)}, f32[128,256]{0,1:T(8,128)S(1)}, s32[]{:T(128)}, s32[]{:T(128)}, /*index=5*/s32[]{:T(128)}, s32[]{:T(128)}) while((s32[]{:T(128)}, f32[128,256]{0,1:T(8,128)S(1)}, f32[128,256]{0,1:T(8,128)S(1)}, s32[]{:T(128)}, s32[]{:T(128)}, /*index=5*/s32[]{:T(128)}, s32[]{:T(128)}) %tuple.197), condition=%wide.region_8.9_spmd.clone, body=%wide.region_7.8_spmd.clone.sunk | while | flops 66180 | bytes 271501 | solution.py:47
  1990.8 1.1 fusion.12
  1992.0 1.1 fusion.16
  (2601 shorter events, 1093.3 us)
Async XLA Ops:
  8.7 29.8 %all-to-all-start = ((bf16[32,256,4]{1,2,0:T(4,128)(2,1)}), bf16[32,256,4]{1,2,0:T(4,128)(2,1)S(1)}, u32[]{:S(2)}, u32[]{:S(2)}) async-start(bf16[32,256,4]{1,2,0:T(4,128)(2,1)} %bitcast.1), calls=%async_computation | async-start | bytes 131072 | tf_op jit(solution)/shard_map/all_to_all | solution.py:103
  25.5 482.1 %all-reduce.3.cloned.1.call-start = ((), (), s32[]{:S(2)}) async-start(), calls=%async_computation.1 | async-start | bytes 2097152 | tf_op jit(solution)/shard_map/psum | solution.py:112
  38.6 5.2 collective-permute-start
Sparse Core Ops, SparseCore 0:
  45.4 462.1 all-reduce.2
where the time goes:
time: 2020 us; the launch traced here: 2000 us
  local copies, waits for them, and re-layouts  614 us (30%)
  other arithmetic  489 us (24%)
  waiting for transfers between devices  476 us (24%)
  loops' own time  377 us (19%)
  starting transfers between devices  20.3 us (1%)
    psum x1, waiting for transfers between devices, shards(): gram = lax.psum(partial_value, ('grp', 'dev'))  462 us
    another operation x4, loops' own time, factor_block(): lax.fori_loop(0, size, eliminate, (augmented, jnp.zeros_like(augmented)))  377 us
    mul x512, other arithmetic, eliminate(): working = working - factor[:, None] * pivot_row[None, :]  337 us
    dynamic_update_slice x512, local copies, waits for them, and re-layouts, eliminate(): written = lax.dynamic_update_slice_in_dim(written, scaled[None, :], step, 0)  312 us
    dynamic_slice x512, local copies, waits for them, and re-layouts, eliminate(): pivot = lax.dynamic_slice_in_dim(pivot_row, step, 1, 0)[0]  301 us
    div x512, other arithmetic, eliminate(): scaled = pivot_row / jnp.sqrt(pivot)  94.6 us
    sub x512, other arithmetic, eliminate(): working = working - factor[:, None] * pivot_row[None, :]  53.9 us
  transfers between devices with their start and end apart: 3, of which 3 were waited for; matrix products, arithmetic and copies ran while one was open for 0% of the time, Pallas kernels for 0%

commit v1 on v0

--- a/solution.py
+++ b/solution.py
@@ -109,7 +109,7 @@
     hankel = jnp.where(valid[:, None], hankel, jnp.zeros_like(hankel))
     total_rows = rows * lax.axis_size("grp") * lax.axis_size("dev")
     partial_value = gram_term(hankel)
-    gram = lax.psum(partial_value, ("grp", "dev"))
+    gram = lax.psum(lax.psum(partial_value, "dev"), "grp")
     upper, inverse = factor_parts(gram / total_rows)
     high = inverse.astype(jnp.bfloat16)
     low = (inverse - lax.optimization_barrier(high).astype(jnp.float32)).astype(jnp.bfloat16)

time: 2020 us -> 1870 us (0.926)
  waiting for transfers between devices: 476 us -> 339 us
    psum x1 -> x2, waiting for transfers between devices: 462 us -> 325 us  [shards(): gram = lax.psum(lax.psum(partial_value, 'dev'), 'grp')]
  transfers between devices with their start and end apart: 3 -> 4, of which waited for: 3 -> 4; matrix products, arithmetic and copies ran while one was open for 0% -> 0% of each run, Pallas kernels for 0% -> 0%
where the time goes in v1:
time: 1870 us; the launch traced here: 1860 us
  local copies, waits for them, and re-layouts  618 us (33%)
  other arithmetic  484 us (26%)
  loops' own time  372 us (20%)
  waiting for transfers between devices  339 us (18%)
  starting transfers between devices  20.3 us (1%)
    another operation x4, loops' own time, factor_block(): lax.fori_loop(0, size, eliminate, (augmented, jnp.zeros_like(augmented)))  372 us
    mul x512, other arithmetic, eliminate(): working = working - factor[:, None] * pivot_row[None, :]  331 us
    psum x2, waiting for transfers between devices, shards(): gram = lax.psum(lax.psum(partial_value, 'dev'), 'grp')  325 us
    dynamic_update_slice x512, local copies, waits for them, and re-layouts, eliminate(): written = lax.dynamic_update_slice_in_dim(written, scaled[None, :], step, 0)  312 us
    dynamic_slice x512, local copies, waits for them, and re-layouts, eliminate(): pivot = lax.dynamic_slice_in_dim(pivot_row, step, 1, 0)[0]  305 us
    div x512, other arithmetic, eliminate(): scaled = pivot_row / jnp.sqrt(pivot)  94.6 us
    sub x512, other arithmetic, eliminate(): working = working - factor[:, None] * pivot_row[None, :]  53.9 us
  transfers between devices with their start and end apart: 4, of which 4 were waited for; matrix products, arithmetic and copies ran while one was open for 0% of the time, Pallas kernels for 0%

profile of v1, /device:TPU:1, one launch (start us, length us, event | category | flops | bytes accessed | tf_op | source)
XLA Modules:
  0.0 1856.8 jit_solution(18017949488529937172)
XLA Ops:
  7.2 1.6 multiply_convert_fusion
  8.7 16.8 all-to-all-start
  26.2 12.4 all-to-all-done
  38.6 3.5 collective-permute-start
  42.1 1.7 collective-permute-done
  44.0 1.3 fusion.66
  45.4 205.5 %all-reduce.4.cloned.1.call-done = f32[512,512]{1,0:T(8,128)} async-done(((f32[512,512]{1,0:T(8,128)}), f32[512,512]{1,0:T(8,128)}) %all-reduce.4.cloned.1.call-update) | async-done | bytes 1048592 | tf_op jit(solution)/shard_map/psum | solution.py:112
  251.0 119.6 %all-reduce.6.cloned.1.call-done = f32[512,512]{1,0:T(8,128)} async-done(((f32[512,512]{1,0:T(8,128)}), f32[512,512]{1,0:T(8,128)}) %all-reduce.6.cloned.1.call-update) | async-done | bytes 1048592 | tf_op jit(solution)/shard_map/psum | solution.py:112
  370.5 1.3 broadcast_multiply_fusion
  372.0 362.4 %while.76 = (s32[]{:T(128)}, f32[128,256]{0,1:T(8,128)S(1)}, f32[128,256]{0,1:T(8,128)S(1)}, s32[]{:T(128)}, s32[]{:T(128)}, /*index=5*/s32[]{:T(128)}, s32[]{:T(128)}) while((s32[]{:T(128)}, f32[128,256]{0,1:T(8,128)S(1)}, f32[128,256]{0,1:T(8,128)S(1)}, s32[]{:T(128)}, s32[]{:T(128)}, /*index=5*/s32[]{:T(128)}, s32[]{:T(128)}) %tuple.188), condition=%wide.region_3.4_spmd.clone, body=%wide.region_2.3_spmd.clone.sunk | while | flops 66180 | bytes 271501 | solution.py:47
  734.9 0.7 convolution_subtract_fusion
  735.7 368.6 %while.77 = (s32[]{:T(128)}, f32[128,256]{0,1:T(8,128)S(1)}, f32[128,256]{0,1:T(8,128)S(1)}, s32[]{:T(128)}, s32[]{:T(128)}, /*index=5*/s32[]{:T(128)}, s32[]{:T(128)}) while((s32[]{:T(128)}, f32[128,256]{0,1:T(8,128)S(1)}, f32[128,256]{0,1:T(8,128)S(1)}, s32[]{:T(128)}, s32[]{:T(128)}, /*index=5*/s32[]{:T(128)}, s32[]{:T(128)}) %tuple.191), condition=%wide.region_5.6_spmd.clone, body=%wide.region_4.5_spmd.clone.sunk | while | flops 66180 | bytes 271501 | solution.py:47
  737.7 0.7 fusion.93
  746.3 0.7 fusion.93
  752.1 0.7 fusion.93
  760.7 0.7 fusion.93
  769.3 0.7 fusion.93
  775.1 0.7 fusion.93
  778.0 0.7 fusion.93
  783.7 0.7 fusion.93
  792.4 0.7 fusion.93
  801.0 0.7 fusion.93
  806.8 0.7 fusion.93
  815.4 0.7 fusion.93
  824.1 0.7 fusion.93
  829.8 0.7 fusion.93
  832.7 0.7 fusion.93
  838.5 0.7 fusion.93
  1105.4 368.6 %while.78 = (s32[]{:T(128)}, f32[128,256]{0,1:T(8,128)S(1)}, f32[128,256]{0,1:T(8,128)S(1)}, s32[]{:T(128)}, s32[]{:T(128)}, /*index=5*/s32[]{:T(128)}, s32[]{:T(128)}) while((s32[]{:T(128)}, f32[128,256]{0,1:T(8,128)S(1)}, f32[128,256]{0,1:T(8,128)S(1)}, s32[]{:T(128)}, s32[]{:T(128)}, /*index=5*/s32[]{:T(128)}, s32[]{:T(128)}) %tuple.194), condition=%wide.region_7.8_spmd.clone, body=%wide.region_6.7_spmd.clone.sunk | while | flops 66180 | bytes 271501 | solution.py:47
  1475.0 368.6 %while.79 = (s32[]{:T(128)}, f32[128,256]{0,1:T(8,128)S(1)}, f32[128,256]{0,1:T(8,128)S(1)}, s32[]{:T(128)}, s32[]{:T(128)}, /*index=5*/s32[]{:T(128)}, s32[]{:T(128)}) while((s32[]{:T(128)}, f32[128,256]{0,1:T(8,128)S(1)}, f32[128,256]{0,1:T(8,128)S(1)}, s32[]{:T(128)}, s32[]{:T(128)}, /*index=5*/s32[]{:T(128)}, s32[]{:T(128)}) %tuple.197), condition=%wide.region_9.10_spmd.clone, body=%wide.region_8.9_spmd.clone.sunk | while | flops 66180 | bytes 271501 | solution.py:47
  1847.7 1.1 fusion.12
  1848.8 1.1 fusion.16
  (2604 shorter events, 1092.8 us)
Async XLA Ops:
  8.7 29.8 %all-to-all-start = ((bf16[32,256,4]{1,2,0:T(4,128)(2,1)}), bf16[32,256,4]{1,2,0:T(4,128)(2,1)S(1)}, u32[]{:S(2)}, u32[]{:S(2)}) async-start(bf16[32,256,4]{1,2,0:T(4,128)(2,1)} %bitcast.1), calls=%async_computation | async-start | bytes 131072 | tf_op jit(solution)/shard_map/all_to_all | solution.py:103
  25.5 225.4 %all-reduce.4.cloned.1.call-start = ((), (), s32[]{:S(2)}) async-start(), calls=%async_computation.1 | async-start | bytes 2097152 | tf_op jit(solution)/shard_map/psum | solution.py:112
  38.6 5.2 collective-permute-start
  45.3 325.2 %all-reduce.6.cloned.1.call-start = ((), (), s32[]{:S(2)}) async-start(), calls=%async_computation.2 | async-start | bytes 2097152 | tf_op jit(solution)/shard_map/psum | solution.py:112
Sparse Core Ops, SparseCore 0:
  45.4 205.4 all-reduce.3
  254.5 116.0 all-reduce.5
